TPU v7x, 32 devices: a whole 2x2x4 slice. The times are simulated.
32 devices in a mesh: dp: 16 (over z, y, core), tensor: 2 (over x).
Axes of the slice: x: 2, y: 2, z: 4, core: 2. Of those that a mesh axis runs over, the one named last changes fastest.
Arguments:
- tokens: bfloat16 [6144, 4096], P(('dp', 'tensor')), may hold values from -21 to 21
- wq_codes: bfloat16 [4096, 1024], P('dp', 'tensor'), may hold values from -4 to 4
- wq_scales: float32 [32, 8], replicated, may hold values from 0.0078125 to 0.03125
- wk_codes: bfloat16 [4096, 128], P('dp', 'tensor'), may hold values from -4 to 4
- wk_scales: float32 [32, 1], replicated, may hold values from 0.0078125 to 0.03125
- wv_codes: bfloat16 [4096, 128], P('dp', 'tensor'), may hold values from -4 to 4
- wv_scales: float32 [32, 1], replicated, may hold values from 0.0078125 to 0.03125
- wo_codes: bfloat16 [1024, 4096], P('tensor', 'dp'), may hold values from -4 to 4
- wo_scales: float32 [8, 32], replicated, may hold values from 0.015625 to 0.0625
Outputs:
- mixed: bfloat16 [6144, 4096], P(('dp', 'tensor'))
All inputs are finite; a program needn't handle non-finite values.
Results may differ from a plain program's by a relative error of at most 0.014.
The roundings to bfloat16 on the way count: a program that leaves them out, or rounds other values in their place, can miss the bound.
Values may be sent and summed in bfloat16 or wider, within the bound.
A program may use at most 64 MiB of HBM per device.

v0:
```python
import jax
import jax.numpy as jnp
from jax import lax
from jax.sharding import PartitionSpec as P

HEAD = 128
BLOCK = 128
SPAN = 384
rope_base = 500000.0
masked_value = -1e30


def from_partner(value, axis, apart):
    mask = 2**apart
    pairs = [(source, source ^ mask) for source in range(lax.axis_size(axis))]
    return lax.ppermute(value, axis, pairs)


def dequantize(codes, scales, row_start, col_start):
    height, breadth = codes.shape
    row_block = (row_start + jnp.arange(height, dtype=jnp.int32)) // BLOCK
    col_block = (col_start + jnp.arange(breadth, dtype=jnp.int32)) // BLOCK
    row_pick = (row_block[:, None] == jnp.arange(scales.shape[0], dtype=jnp.int32)[None, :]).astype(
        jnp.float32
    )
    col_pick = (col_block[None, :] == jnp.arange(scales.shape[1], dtype=jnp.int32)[:, None]).astype(
        jnp.float32
    )
    picked = jnp.dot(row_pick, scales, precision=lax.Precision.HIGHEST)
    expanded = jnp.dot(picked, col_pick, precision=lax.Precision.HIGHEST)
    return (codes.astype(jnp.float32) * expanded).astype(jnp.bfloat16)


def rotate(features, positions):
    half_size = HEAD // 2
    steps = jnp.arange(half_size).astype(jnp.float32)
    inverse = jnp.exp(-(2.0 * steps / HEAD) * jnp.log(jnp.float32(rope_base)))
    angle = positions[:, None] * inverse[None, :]
    cosine = jnp.cos(angle)[:, None, :]
    sine = jnp.sin(angle)[:, None, :]
    first = features[..., :half_size]
    second = features[..., half_size:]
    return jnp.concatenate(
        [first * cosine - second * sine, second * cosine + first * sine], axis=-1
    )


def in_order(upper, mine, partner):
    return jnp.where(
        upper, jnp.concatenate([partner, mine], axis=1), jnp.concatenate([mine, partner], axis=1)
    )


def body(
    tokens, wq_codes, wq_scales, wk_codes, wk_scales, wv_codes, wv_scales, wo_codes, wo_scales
):
    data_index = lax.axis_index("dp")
    head_index = lax.axis_index("tensor")
    weight_rows = wq_codes.shape[0]
    row_start = data_index * weight_rows
    query_width = wq_codes.shape[1]
    shard_width = wk_codes.shape[1]
    wq_local = dequantize(wq_codes, wq_scales, row_start, head_index * query_width)
    wk_local = dequantize(wk_codes, wk_scales, row_start, head_index * shard_width)
    wv_local = dequantize(wv_codes, wv_scales, row_start, head_index * shard_width)
    wo_local = dequantize(
        wo_codes, wo_scales, head_index * wo_codes.shape[0], data_index * wo_codes.shape[1]
    )
    wo_whole = lax.all_gather(wo_local, "dp", axis=1, tiled=True)
    sequence = lax.all_gather(tokens, "tensor", axis=0, tiled=True)
    upper = head_index % 2 == 1
    partner_k, partner_v = from_partner((wk_local, wv_local), "tensor", 0)
    wk_used = in_order(upper, wk_local, partner_k)
    wv_used = in_order(upper, wv_local, partner_v)
    length = sequence.shape[0]
    full_q, full_k, full_v = (
        lax.all_gather(wq_local, "dp", axis=0, tiled=True),
        lax.all_gather(wk_used, "dp", axis=0, tiled=True),
        lax.all_gather(wv_used, "dp", axis=0, tiled=True),
    )
    query_lin = jnp.dot(sequence, full_q, preferred_element_type=jnp.float32)
    key_lin = jnp.dot(sequence, full_k, preferred_element_type=jnp.float32)
    value_lin = jnp.dot(sequence, full_v, preferred_element_type=jnp.float32)
    positions = (jnp.arange(length) % SPAN).astype(jnp.float32)
    heads_here = query_width // HEAD
    span_count = length // SPAN
    queries = rotate(query_lin.reshape(length, heads_here, HEAD), positions).astype(jnp.bfloat16)
    keys = rotate(key_lin.reshape(length, 1, HEAD), positions)[:, 0, :].astype(jnp.bfloat16)
    values = value_lin.astype(jnp.bfloat16)
    queries = queries.reshape(span_count, SPAN, heads_here, HEAD)
    keys = keys.reshape(span_count, SPAN, HEAD)
    values = values.reshape(span_count, SPAN, HEAD)
    causal = jnp.arange(SPAN)[:, None] >= jnp.arange(SPAN)[None, :]
    scores = jnp.einsum("cqhd,ckd->chqk", queries, keys, preferred_element_type=jnp.float32) * (
        1.0 / HEAD**0.5
    )
    scores = jnp.where(causal[None, None, :, :], scores, masked_value)
    peak = jnp.max(scores, axis=-1, keepdims=True)
    powers = jnp.exp(scores - peak)
    total = jnp.sum(powers, axis=-1, keepdims=True)
    probs = (powers / total).astype(jnp.bfloat16)
    attended = (
        jnp.einsum("chqk,ckd->cqhd", probs, values, preferred_element_type=jnp.float32)
        .astype(jnp.bfloat16)
        .reshape(length, query_width)
    )
    terms = jnp.dot(attended, wo_whole, preferred_element_type=jnp.float32)
    mixed = lax.psum_scatter(terms.astype(jnp.bfloat16), "tensor", scatter_dimension=0, tiled=True)
    return mixed


def solution(mesh):
    return jax.shard_map(
        body,
        mesh=mesh,
        in_specs=(
            P(("dp", "tensor"), None),
            P("dp", "tensor"),
            P(),
            P("dp", "tensor"),
            P(),
            P("dp", "tensor"),
            P(),
            P("tensor", "dp"),
            P(),
        ),
        out_specs=P(("dp", "tensor"), None),
        check_vma=False,
    )
```

profile of v0, /device:TPU:0, one launch (start us, length us, event | category | flops | bytes accessed | tf_op | source)
XLA Modules:
  0.0 298.7 jit_solution(14492165854905876810)
XLA Ops:
  6.6 0.9 fusion.18
  7.5 0.9 fusion.17
  8.4 0.9 multiply_convert_fusion.1
  9.3 3.0 %collective-permute-start.1 = (bf16[256,64]{0,1:T(8,128)(2,1)S(1)}, bf16[256,64]{0,1:T(8,128)(2,1)S(1)}, u32[]{:S(2)}, u32[]{:S(2)}) collective-permute-start(bf16[256,64]{0,1:T(8,128)(2,1)S(1)} %get-tuple-element.14), channel_id=1, source_target_pairs={{0,1},{1,0},{2,3},{3,2},{4,5},{5,4},{6,7},{7,6},{8,9},{9,8},{10,11... | collective-permute-start | bytes 98312 | tf_op jit(solution)/shard_map/ppermute | solution.py:16
  12.3 1.9 collective-permute-done.1
  14.2 0.6 maximum_select_fusion.1
  14.9 0.7 all-gather.8.cloned.1.call-update
  15.7 0.9 fusion.16
  16.7 1.1 fusion.2
  17.8 2.1 collective-permute-start
  19.9 1.9 collective-permute-done
  21.8 0.6 maximum_select_fusion
  22.5 0.3 fusion.10
  22.8 1.1 fusion.3
  24.1 1.4 multiply_cosine_fusion
  25.5 28.1 %all-gather.10.cloned.1.call-done = bf16[4096,128]{0,1:T(8,128)(2,1)} async-done(((bf16[256,128]{0,1:T(8,128)(2,1)}), bf16[4096,128]{0,1:T(8,128)(2,1)}) %all-gather.10.cloned.1.call-update) | async-done | bytes 1048592 | tf_op jit(solution)/shard_map/all_gather | solution.py:78
  53.6 46.0 %all-gather.8.cloned.1.call-done = bf16[384,4096]{1,0:T(8,128)(2,1)} async-done(((bf16[192,4096]{1,0:T(8,128)(2,1)}), bf16[384,4096]{1,0:T(8,128)(2,1)}) %all-gather.8.cloned.1.call-update) | async-done | bytes 3145744 | tf_op jit(solution)/shard_map/all_gather | solution.py:70
  99.6 3.4 %convolution_bitcast_fusion = f32[384,1,128]{0,2,1:T(8,128)S(1)} fusion(bf16[4096,128]{0,1:T(8,128)(2,1)} %all-gather.10.cloned.1.call-done, bf16[384,4096]{1,0:T(8,128)(2,1)} %all-gather.8.cloned.1.call-done), kind=kOutput, calls=%fused_computation.12 | convolution fusion | flops 402653184 | bytes 4390912 | tf_op jit(solution)/shard_map/dot_general | solution.py:82
  103.1 1.1 fusion.20
  104.1 48.3 %all-gather.12.cloned.1.call-done = bf16[4096,512]{1,0:T(8,128)(2,1)} async-done(((bf16[256,512]{1,0:T(8,128)(2,1)}), bf16[4096,512]{1,0:T(8,128)(2,1)}) %all-gather.12.cloned.1.call-update) | async-done | bytes 4194320 | tf_op jit(solution)/shard_map/all_gather | solution.py:77
  152.4 4.6 %fusion.37 = f32[512,384]{1,0:T(8,128)S(1)} fusion(bf16[4096,512]{1,0:T(8,128)(2,1)} %all-gather.12.cloned.1.call-done, bf16[384,4096]{1,0:T(8,128)(2,1)S(1)} %copy-done.1), kind=kOutput, calls=%fused_computation.79 | convolution fusion | flops 1610612736 | bytes 8126464 | tf_op jit(solution)/shard_map/dot_general | solution.py:81
  157.1 0.3 copy.17
  157.4 0.3 copy.18
  157.6 0.3 copy-done.2
  157.9 0.2 subtract_convert_fusion
  158.2 0.7 fusion.1
  158.9 0.5 fusion
  159.4 30.4 %all-gather.6.cloned.1.call-done = bf16[4096,128]{0,1:T(8,128)(2,1)} async-done(((bf16[256,128]{0,1:T(8,128)(2,1)}), bf16[4096,128]{0,1:T(8,128)(2,1)}) %all-gather.6.cloned.1.call-update) | async-done | bytes 1048592 | tf_op jit(solution)/shard_map/all_gather | solution.py:79
  189.7 4.1 %convolution_convert_fusion.1 = bf16[128,4,384]{2,0,1:T(8,128)(2,1)S(1)} fusion(f32[384,384,4]{1,0,2:T(8,128)S(1)} %get-tuple-element.16, f32[4,384]{1,0:T(4,128)S(1)} %fusion, f32[4,384]{1,0:T(4,128)S(1)} %get-tuple-element.15, pred[384,384]{0,1:T(8,128)(4,1)S(1)} %iota_compare_fusion, bf16[4096,128]{0,1:T(8,128)(2,1)} %all-gather.6.cloned.1.call-done, ...), kind=kOutput, calls=%fused_computation.6 | convolution fusion | flops 556843008 | bytes 7106560 | tf_op jit(solution)/shard_map/chqk,ckd->cqhd/dot_general | solution.py:103
  193.8 50.7 %all-gather.14.cloned.1.call-done = bf16[512,4096]{1,0:T(8,128)(2,1)} async-done(((bf16[512,256]{1,0:T(8,128)(2,1)}), bf16[512,4096]{1,0:T(8,128)(2,1)}) %all-gather.14.cloned.1.call-update) | async-done | bytes 4194320 | tf_op jit(solution)/shard_map/all_gather | solution.py:69
  244.5 5.7 %convolution_convert_fusion = bf16[384,4096]{1,0:T(8,128)(2,1)} fusion(bf16[384,512]{0,1:T(8,128)(2,1)S(1)} %bitcast.58, bf16[512,4096]{1,0:T(8,128)(2,1)} %all-gather.14.cloned.1.call-done), kind=kOutput, calls=%fused_computation | convolution fusion | flops 1612185600 | bytes 7733248 | tf_op jit(solution)/shard_map/dot_general | solution.py:107
  250.2 41.7 %reduce-scatter.2.cloned.1.call-done = bf16[192,4096]{1,0:T(8,128)(2,1)} async-done(((bf16[384,4096]{1,0:T(8,128)(2,1)}), bf16[192,4096]{1,0:T(8,128)(2,1)}) %reduce-scatter.2.cloned.1.call-update) | async-done | bytes 1572880 | tf_op jit(solution)/shard_map/reduce_scatter | solution.py:108
  (29 shorter events, 0.5 us)
Async XLA Ops:
  6.5 16.0 %copy-start = (f32[8,32]{1,0:T(8,128)S(1)}, f32[8,32]{1,0:T(8,128)}, u32[]{:S(2)}) copy-start(f32[8,32]{1,0:T(8,128)} %param.17) | copy-start | bytes 3076
  6.5 10.1 %copy-start.3 = (bf16[256,512]{1,0:T(8,128)(2,1)S(1)}, bf16[256,512]{1,0:T(8,128)(2,1)}, u32[]{:S(2)}) copy-start(bf16[256,512]{1,0:T(8,128)(2,1)} %param.10) | copy-start | bytes 786436
  6.5 16.3 %copy-start.4 = (bf16[512,256]{1,0:T(8,128)(2,1)S(1)}, bf16[512,256]{1,0:T(8,128)(2,1)}, u32[]{:S(2)}) copy-start(bf16[512,256]{1,0:T(8,128)(2,1)} %param.16) | copy-start | bytes 786436
  6.5 47.1 %all-gather.10.cloned.1.call-start = ((), (), s32[]{:S(2)}) async-start(), calls=%async_computation.3 | async-start | bytes 1114112 | tf_op jit(solution)/shard_map/all_gather | solution.py:78
  9.3 4.9 %collective-permute-start.1 = (bf16[256,64]{0,1:T(8,128)(2,1)S(1)}, bf16[256,64]{0,1:T(8,128)(2,1)S(1)}, u32[]{:S(2)}, u32[]{:S(2)}) collective-permute-start(bf16[256,64]{0,1:T(8,128)(2,1)S(1)} %get-tuple-element.14), channel_id=1, source_target_pairs={{0,1},{1,0},{2,3},{3,2},{4,5},{5,4},{6,7},{7,6},{8,9},{9,8},{10,11... | collective-permute-start | bytes 98312 | tf_op jit(solution)/shard_map/ppermute | solution.py:16
  14.9 84.7 %all-gather.8.cloned.1.call-start = ((), (), s32[]{:S(2)}) async-start(), calls=%async_computation.2 | async-start | bytes 4718592 | tf_op jit(solution)/shard_map/all_gather | solution.py:70
  15.6 136.8 %all-gather.12.cloned.1.call-start = ((), (), s32[]{:S(2)}) async-start(), calls=%async_computation.4 | async-start | bytes 4456448 | tf_op jit(solution)/shard_map/all_gather | solution.py:77
  17.8 172.0 %all-gather.6.cloned.1.call-start = ((), (), s32[]{:S(2)}) async-start(), calls=%async_computation.1 | async-start | bytes 1114112 | tf_op jit(solution)/shard_map/all_gather | solution.py:79
  17.8 4.0 %collective-permute-start = (bf16[256,64]{0,1:T(8,128)(2,1)S(1)}, bf16[256,64]{0,1:T(8,128)(2,1)S(1)}, u32[]{:S(2)}, u32[]{:S(2)}) collective-permute-start(bf16[256,64]{0,1:T(8,128)(2,1)S(1)} %get-tuple-element.13), channel_id=1, source_target_pairs={{0,1},{1,0},{2,3},{3,2},{4,5},{5,4},{6,7},{7,6},{8,9},{9,8},{10,11... | collective-permute-start | bytes 98312 | tf_op jit(solution)/shard_map/ppermute | solution.py:16
  22.4 222.0 %all-gather.14.cloned.1.call-start = ((), (), s32[]{:S(2)}) async-start(), calls=%async_computation.5 | async-start | bytes 4456448 | tf_op jit(solution)/shard_map/all_gather | solution.py:69
  23.9 267.9 %reduce-scatter.2.cloned.1.call-start = ((), (), s32[]{:S(2)}) async-start(), calls=%async_computation.6 | async-start | bytes 4718592 | tf_op jit(solution)/shard_map/reduce_scatter | solution.py:108
  99.6 52.8 %copy-start.1 = (bf16[384,4096]{1,0:T(8,128)(2,1)S(1)}, bf16[384,4096]{1,0:T(8,128)(2,1)}, u32[]{:S(2)}) copy-start(bf16[384,4096]{1,0:T(8,128)(2,1)} %all-gather.8.cloned.1.call-done) | copy-start | bytes 9437188
  157.0 0.9 copy-start.2
  157.1 1.1 copy-start.5
Sparse Core Ops, SparseCore 0:
  15.0 38.5 all-gather.9
  55.2 44.4 all-gather.7
  101.8 50.5 all-gather.11
  154.4 35.2 all-gather.5
  191.7 52.6 all-gather.13
  250.3 41.4 reduce-scatter.1
where the time goes:
time: 299 us
  waiting for transfers between devices  250 us (84%)
  matrix products  23.7 us (8%)
  between operations  13.7 us (5%)
  other arithmetic  5.51 us (2%)
  starting transfers between devices  5.3 us (2%)
    all_gather x1, waiting for transfers between devices, body(): wo_whole = lax.all_gather(wo_local, 'dp', axis=1, tiled=True)  50.7 us
    all_gather x1, waiting for transfers between devices, body(): lax.all_gather(wq_local, 'dp', axis=0, tiled=True)  48.3 us
    all_gather x1, waiting for transfers between devices, body(): sequence = lax.all_gather(tokens, 'tensor', axis=0, tiled=True)  46 us
    reduce_scatter x1, waiting for transfers between devices, body(): lax.psum_scatter(terms.astype(jnp.bfloat16), 'tensor', scatter_dimension=...  41.7 us
    all_gather x1, waiting for transfers between devices, body(): lax.all_gather(wv_used, 'dp', axis=0, tiled=True)  30.4 us
    all_gather x1, waiting for transfers between devices, body(): lax.all_gather(wk_used, 'dp', axis=0, tiled=True)  28.1 us
  transfers between devices with their start and end apart: 8, of which 8 were waited for; matrix products, arithmetic and copies ran while one was open for 7% of the time, Pallas kernels for 0%

commit v1 on v0

--- a/solution.py
+++ b/solution.py
@@ -66,7 +66,12 @@
     wo_local = dequantize(
         wo_codes, wo_scales, head_index * wo_codes.shape[0], data_index * wo_codes.shape[1]
     )
-    wo_whole = lax.all_gather(wo_local, "dp", axis=1, tiled=True)
+    ring = [wo_local]
+    for hop in range(15):
+        ring.append(lax.ppermute(ring[-1], "dp", [(dev, (dev + 1) % 16) for dev in range(16)]))
+    wo_whole = jnp.roll(
+        jnp.concatenate(ring[::-1], axis=1), (lax.axis_index("dp") + 1) * ring[0].shape[1], axis=1
+    )
     sequence = lax.all_gather(tokens, "tensor", axis=0, tiled=True)
     upper = head_index % 2 == 1
     partner_k, partner_v = from_partner((wk_local, wv_local), "tensor", 0)

time: 299 us -> 269 us (0.90)
  waiting for transfers between devices: 250 us -> 176 us
  local copies, waits for them, and re-layouts: 0.91 us -> 42.8 us
    ppermute x0 -> x15, waiting for transfers between devices: none -> 133 us  [body(): lax.ppermute(ring[-1], 'dp', [(dev, (dev + 1) % 16) for dev in range(16)])]
    all_gather x1 -> x0, waiting for transfers between devices: 50.7 us -> none  [body(): wo_whole = lax.all_gather(wo_local, 'dp', axis=1, tiled=True)]
    all_gather x1, waiting for transfers between devices: 48.3 us -> 0.01 us  [body(): lax.all_gather(wq_local, 'dp', axis=0, tiled=True)]
    all_gather x1, waiting for transfers between devices: 46 us -> 0.01 us  [body(): sequence = lax.all_gather(tokens, 'tensor', axis=0, tiled=True)]
    unnamed x14 -> x90, local copies, waits for them, and re-layouts: 0.85 us -> 42 us
    all_gather x1, waiting for transfers between devices: 30.4 us -> 0.02 us  [body(): lax.all_gather(wv_used, 'dp', axis=0, tiled=True)]
    all_gather x1, waiting for transfers between devices: 28.1 us -> 0.01 us  [body(): lax.all_gather(wk_used, 'dp', axis=0, tiled=True)]
  transfers between devices with their start and end apart: 8 -> 22, of which waited for: 8 -> 17; matrix products, arithmetic and copies ran while one was open for 7% -> 19% of each run, Pallas kernels for 0% -> 0%
where the time goes in v1:
time: 269 us
  waiting for transfers between devices  176 us (65%)
  local copies, waits for them, and re-layouts  42.8 us (16%)
  matrix products  24.1 us (9%)
  between operations  13.4 us (5%)
  other arithmetic  6.7 us (2%)
  starting transfers between devices  5.64 us (2%)
    ppermute x15, waiting for transfers between devices, body(): lax.ppermute(ring[-1], 'dp', [(dev, (dev + 1) % 16) for dev in range(16)])  133 us
    unnamed x90, local copies, waits for them, and re-layouts  42 us
    reduce_scatter x1, waiting for transfers between devices, body(): lax.psum_scatter(terms.astype(jnp.bfloat16), 'tensor', scatter_dimension=...  40.7 us
    dot_general x1, matrix products, body(): terms = jnp.dot(attended, wo_whole, preferred_element_type=jnp.float32)  5.74 us
    ppermute x2, starting transfers between devices, from_partner(): return lax.ppermute(value, axis, pairs)  5.38 us
  transfers between devices with their start and end apart: 22, of which 17 were waited for; matrix products, arithmetic and copies ran while one was open for 19% of the time, Pallas kernels for 0%

profile of v1, /device:TPU:0, one launch (start us, length us, event | category | flops | bytes accessed | tf_op | source)
XLA Modules:
  0.0 268.7 jit_solution(7116009893303308626)
XLA Ops:
  9.3 3.0 %collective-permute-start.1 = (bf16[256,64]{0,1:T(8,128)(2,1)S(1)}, bf16[256,64]{0,1:T(8,128)(2,1)S(1)}, u32[]{:S(2)}, u32[]{:S(2)}) collective-permute-start(bf16[256,64]{0,1:T(8,128)(2,1)S(1)} %get-tuple-element.14), channel_id=1, source_target_pairs={{0,1},{1,0},{2,3},{3,2},{4,5},{5,4},{6,7},{7,6},{8,9},{9,8},{10,11... | collective-permute-start | bytes 98312 | tf_op jit(solution)/shard_map/ppermute | solution.py:16
  12.3 1.9 collective-permute-done.1
  16.6 2.0 fusion.3
  20.6 8.6 %collective-permute-done.2 = bf16[512,256]{0,1:T(8,128)(2,1)S(1)} collective-permute-done((bf16[512,256]{0,1:T(8,128)(2,1)S(1)}, bf16[512,256]{0,1:T(8,128)(2,1)S(1)}, u32[]{:S(2)}, u32[]{:S(2)}) %collective-permute-start.2) | collective-permute-done | bytes 262176 | tf_op jit(solution)/shard_map/ppermute | solution.py:71
  29.9 8.8 %collective-permute-done.3 = bf16[512,256]{0,1:T(8,128)(2,1)S(1)} collective-permute-done((bf16[512,256]{0,1:T(8,128)(2,1)S(1)}, bf16[512,256]{0,1:T(8,128)(2,1)S(1)}, u32[]{:S(2)}, u32[]{:S(2)}) %collective-permute-start.3) | collective-permute-done | bytes 262176 | tf_op jit(solution)/shard_map/ppermute | solution.py:71
  39.5 10.0 %collective-permute-done.4 = bf16[512,256]{0,1:T(8,128)(2,1)S(1)} collective-permute-done((bf16[512,256]{0,1:T(8,128)(2,1)S(1)}, bf16[512,256]{0,1:T(8,128)(2,1)S(1)}, u32[]{:S(2)}, u32[]{:S(2)}) %collective-permute-start.4) | collective-permute-done | bytes 262176 | tf_op jit(solution)/shard_map/ppermute | solution.py:71
  50.2 8.5 %collective-permute-done.5 = bf16[512,256]{0,1:T(8,128)(2,1)S(1)} collective-permute-done((bf16[512,256]{0,1:T(8,128)(2,1)S(1)}, bf16[512,256]{0,1:T(8,128)(2,1)S(1)}, u32[]{:S(2)}, u32[]{:S(2)}) %collective-permute-start.5) | collective-permute-done | bytes 262176 | tf_op jit(solution)/shard_map/ppermute | solution.py:71
  59.4 8.5 %collective-permute-done.6 = bf16[512,256]{0,1:T(8,128)(2,1)S(1)} collective-permute-done((bf16[512,256]{0,1:T(8,128)(2,1)S(1)}, bf16[512,256]{0,1:T(8,128)(2,1)S(1)}, u32[]{:S(2)}, u32[]{:S(2)}) %collective-permute-start.6) | collective-permute-done | bytes 262176 | tf_op jit(solution)/shard_map/ppermute | solution.py:71
  68.6 8.5 %collective-permute-done.7 = bf16[512,256]{0,1:T(8,128)(2,1)S(1)} collective-permute-done((bf16[512,256]{0,1:T(8,128)(2,1)S(1)}, bf16[512,256]{0,1:T(8,128)(2,1)S(1)}, u32[]{:S(2)}, u32[]{:S(2)}) %collective-permute-start.7) | collective-permute-done | bytes 262176 | tf_op jit(solution)/shard_map/ppermute | solution.py:71
  77.8 8.5 %collective-permute-done.8 = bf16[512,256]{0,1:T(8,128)(2,1)S(1)} collective-permute-done((bf16[512,256]{0,1:T(8,128)(2,1)S(1)}, bf16[512,256]{0,1:T(8,128)(2,1)S(1)}, u32[]{:S(2)}, u32[]{:S(2)}) %collective-permute-start.8) | collective-permute-done | bytes 262176 | tf_op jit(solution)/shard_map/ppermute | solution.py:71
  87.0 8.5 %collective-permute-done.9 = bf16[512,256]{0,1:T(8,128)(2,1)S(1)} collective-permute-done((bf16[512,256]{0,1:T(8,128)(2,1)S(1)}, bf16[512,256]{0,1:T(8,128)(2,1)S(1)}, u32[]{:S(2)}, u32[]{:S(2)}) %collective-permute-start.9) | collective-permute-done | bytes 262176 | tf_op jit(solution)/shard_map/ppermute | solution.py:71
  96.2 8.5 %collective-permute-done.10 = bf16[512,256]{0,1:T(8,128)(2,1)S(1)} collective-permute-done((bf16[512,256]{0,1:T(8,128)(2,1)S(1)}, bf16[512,256]{0,1:T(8,128)(2,1)S(1)}, u32[]{:S(2)}, u32[]{:S(2)}) %collective-permute-start.10) | collective-permute-done | bytes 262176 | tf_op jit(solution)/shard_map/ppermute | solution.py:71
  105.4 8.5 %collective-permute-done.11 = bf16[512,256]{0,1:T(8,128)(2,1)S(1)} collective-permute-done((bf16[512,256]{0,1:T(8,128)(2,1)S(1)}, bf16[512,256]{0,1:T(8,128)(2,1)S(1)}, u32[]{:S(2)}, u32[]{:S(2)}) %collective-permute-start.11) | collective-permute-done | bytes 262176 | tf_op jit(solution)/shard_map/ppermute | solution.py:71
  114.6 14.0 %collective-permute-done.12 = bf16[512,256]{0,1:T(8,128)(2,1)S(1)} collective-permute-done((bf16[512,256]{0,1:T(8,128)(2,1)S(1)}, bf16[512,256]{0,1:T(8,128)(2,1)S(1)}, u32[]{:S(2)}, u32[]{:S(2)}) %collective-permute-start.12) | collective-permute-done | bytes 262176 | tf_op jit(solution)/shard_map/ppermute | solution.py:71
  129.3 8.7 %collective-permute-done.13 = bf16[512,256]{0,1:T(8,128)(2,1)S(1)} collective-permute-done((bf16[512,256]{0,1:T(8,128)(2,1)S(1)}, bf16[512,256]{0,1:T(8,128)(2,1)S(1)}, u32[]{:S(2)}, u32[]{:S(2)}) %collective-permute-start.13) | collective-permute-done | bytes 262176 | tf_op jit(solution)/shard_map/ppermute | solution.py:71
  138.7 2.4 collective-permute-start
  141.1 10.5 %collective-permute-done.14 = bf16[512,256]{0,1:T(8,128)(2,1)S(1)} collective-permute-done((bf16[512,256]{0,1:T(8,128)(2,1)S(1)}, bf16[512,256]{0,1:T(8,128)(2,1)S(1)}, u32[]{:S(2)}, u32[]{:S(2)}) %collective-permute-start.14) | collective-permute-done | bytes 262176 | tf_op jit(solution)/shard_map/ppermute | solution.py:71
  154.5 7.8 %collective-permute-done.15 = bf16[512,256]{0,1:T(8,128)(2,1)} collective-permute-done((bf16[512,256]{0,1:T(8,128)(2,1)S(1)}, bf16[512,256]{0,1:T(8,128)(2,1)}, u32[]{:S(2)}, u32[]{:S(2)}) %collective-permute-start.15) | collective-permute-done | bytes 262176 | tf_op jit(solution)/shard_map/ppermute | solution.py:71
  162.4 3.4 %convolution_bitcast_fusion = f32[384,1,128]{0,2,1:T(8,128)S(1)} fusion(bf16[4096,128]{0,1:T(8,128)(2,1)} %all-gather.9.cloned.1.call-done, bf16[384,4096]{1,0:T(8,128)(2,1)} %all-gather.7.cloned.1.call-done), kind=kOutput, calls=%fused_computation.13 | convolution fusion | flops 402653184 | bytes 4390912 | tf_op jit(solution)/shard_map/dot_general | solution.py:87
  166.3 4.8 %collective-permute-done.16 = bf16[512,256]{0,1:T(8,128)(2,1)} collective-permute-done((bf16[512,256]{0,1:T(8,128)(2,1)}, bf16[512,256]{0,1:T(8,128)(2,1)}, u32[]{:S(2)}, u32[]{:S(2)}) %collective-permute-start.16) | collective-permute-done | bytes 262176 | tf_op jit(solution)/shard_map/ppermute | solution.py:71
  171.1 1.7 constant_dynamic-update-slice_fusion.31
  172.8 1.7 constant_dynamic-update-slice_fusion.30
  174.5 1.7 constant_dynamic-update-slice_fusion.29
  177.8 1.7 constant_dynamic-update-slice_fusion.27
  179.5 1.7 constant_dynamic-update-slice_fusion.26
  181.1 1.7 constant_dynamic-update-slice_fusion.25
  190.9 1.7 constant_dynamic-update-slice_fusion.14
  195.5 1.7 constant_dynamic-update-slice_fusion.9
  203.8 4.6 %fusion.39 = f32[512,384]{1,0:T(8,128)S(1)} fusion(bf16[4096,512]{1,0:T(8,128)(2,1)} %all-gather.11.cloned.1.call-done, bf16[384,4096]{1,0:T(8,128)(2,1)S(1)} %copy-done.1), kind=kOutput, calls=%fused_computation.113 | convolution fusion | flops 1610612736 | bytes 8126464 | tf_op jit(solution)/shard_map/dot_general | solution.py:86
  211.6 4.1 %convolution_convert_fusion.1 = bf16[128,4,384]{2,0,1:T(8,128)(2,1)S(1)} fusion(f32[384,384,4]{1,0,2:T(8,128)S(1)} %get-tuple-element.16, f32[4,384]{1,0:T(4,128)S(1)} %fusion.1, f32[4,384]{1,0:T(4,128)S(1)} %get-tuple-element.15, pred[384,384]{0,1:T(8,128)(4,1)S(1)} %copy-done.2, bf16[4096,128]{0,1:T(8,128)(2,1)} %all-gather.5.cloned.1.call-done, ...), kind=kOutput, calls=%fused_computation.7 | convolution fusion | flops 556843008 | bytes 7106560 | tf_op jit(solution)/shard_map/chqk,ckd->cqhd/dot_general | solution.py:108
  215.7 5.7 %convolution_convert_fusion = bf16[384,4096]{1,0:T(8,128)(2,1)} fusion(bf16[384,512]{0,1:T(8,128)(2,1)S(1)} %bitcast.59, bf16[512,8192]{0,1:T(8,128)(2,1)} %constant_dynamic-update-slice_fusion, s32[]{:T(128)S(6)} %select_n.88), kind=kOutput, calls=%fused_computation | convolution fusion | flops 1612185600 | bytes 7733252 | tf_op jit(solution)/shard_map/dot_general | solution.py:112
  221.4 40.7 %reduce-scatter.2.cloned.1.call-done = bf16[192,4096]{1,0:T(8,128)(2,1)} async-done(((bf16[384,4096]{1,0:T(8,128)(2,1)}), bf16[192,4096]{1,0:T(8,128)(2,1)}) %reduce-scatter.2.cloned.1.call-update) | async-done | bytes 1572880 | tf_op jit(solution)/shard_map/reduce_scatter | solution.py:113
  (133 shorter events, 41.3 us)
Async XLA Ops:
  6.5 155.8 %all-gather.9.cloned.1.call-start = ((), (), s32[]{:S(2)}) async-start(), calls=%async_computation.3 | async-start | bytes 1114112 | tf_op jit(solution)/shard_map/all_gather | solution.py:83
  9.3 4.9 %collective-permute-start.1 = (bf16[256,64]{0,1:T(8,128)(2,1)S(1)}, bf16[256,64]{0,1:T(8,128)(2,1)S(1)}, u32[]{:S(2)}, u32[]{:S(2)}) collective-permute-start(bf16[256,64]{0,1:T(8,128)(2,1)S(1)} %get-tuple-element.14), channel_id=1, source_target_pairs={{0,1},{1,0},{2,3},{3,2},{4,5},{5,4},{6,7},{7,6},{8,9},{9,8},{10,11... | collective-permute-start | bytes 98312 | tf_op jit(solution)/shard_map/ppermute | solution.py:16
  14.8 147.5 %all-gather.7.cloned.1.call-start = ((), (), s32[]{:S(2)}) async-start(), calls=%async_computation.2 | async-start | bytes 4718592 | tf_op jit(solution)/shard_map/all_gather | solution.py:75
  15.6 188.2 %all-gather.11.cloned.1.call-start = ((), (), s32[]{:S(2)}) async-start(), calls=%async_computation.4 | async-start | bytes 4456448 | tf_op jit(solution)/shard_map/all_gather | solution.py:82
  18.6 192.9 %all-gather.5.cloned.1.call-start = ((), (), s32[]{:S(2)}) async-start(), calls=%async_computation.1 | async-start | bytes 1114112 | tf_op jit(solution)/shard_map/all_gather | solution.py:84
  20.6 8.7 %collective-permute-start.2 = (bf16[512,256]{0,1:T(8,128)(2,1)S(1)}, bf16[512,256]{0,1:T(8,128)(2,1)S(1)}, u32[]{:S(2)}, u32[]{:S(2)}) collective-permute-start(bf16[512,256]{0,1:T(8,128)(2,1)S(1)} %fusion.4), channel_id=1, source_target_pairs={{0,2},{2,4},{4,6},{6,8},{8,10},{10,12},{12,14},{14,16},{16,18},{18... | collective-permute-start | bytes 786440 | tf_op jit(solution)/shard_map/ppermute | solution.py:71
  29.9 8.8 %collective-permute-start.3 = (bf16[512,256]{0,1:T(8,128)(2,1)S(1)}, bf16[512,256]{0,1:T(8,128)(2,1)S(1)}, u32[]{:S(2)}, u32[]{:S(2)}) collective-permute-start(bf16[512,256]{0,1:T(8,128)(2,1)S(1)} %collective-permute-done.2), channel_id=1, source_target_pairs={{0,2},{2,4},{4,6},{6,8},{8,10},{10,12},{12,14},{14,16},{16,18},{18... | collective-permute-start | bytes 786440 | tf_op jit(solution)/shard_map/ppermute | solution.py:71
  39.5 10.0 %collective-permute-start.4 = (bf16[512,256]{0,1:T(8,128)(2,1)S(1)}, bf16[512,256]{0,1:T(8,128)(2,1)S(1)}, u32[]{:S(2)}, u32[]{:S(2)}) collective-permute-start(bf16[512,256]{0,1:T(8,128)(2,1)S(1)} %collective-permute-done.3), channel_id=1, source_target_pairs={{0,2},{2,4},{4,6},{6,8},{8,10},{10,12},{12,14},{14,16},{16,18},{18... | collective-permute-start | bytes 786440 | tf_op jit(solution)/shard_map/ppermute | solution.py:71
  50.2 8.5 %collective-permute-start.5 = (bf16[512,256]{0,1:T(8,128)(2,1)S(1)}, bf16[512,256]{0,1:T(8,128)(2,1)S(1)}, u32[]{:S(2)}, u32[]{:S(2)}) collective-permute-start(bf16[512,256]{0,1:T(8,128)(2,1)S(1)} %collective-permute-done.4), channel_id=1, source_target_pairs={{0,2},{2,4},{4,6},{6,8},{8,10},{10,12},{12,14},{14,16},{16,18},{18... | collective-permute-start | bytes 786440 | tf_op jit(solution)/shard_map/ppermute | solution.py:71
  59.4 8.5 %collective-permute-start.6 = (bf16[512,256]{0,1:T(8,128)(2,1)S(1)}, bf16[512,256]{0,1:T(8,128)(2,1)S(1)}, u32[]{:S(2)}, u32[]{:S(2)}) collective-permute-start(bf16[512,256]{0,1:T(8,128)(2,1)S(1)} %collective-permute-done.5), channel_id=1, source_target_pairs={{0,2},{2,4},{4,6},{6,8},{8,10},{10,12},{12,14},{14,16},{16,18},{18... | collective-permute-start | bytes 786440 | tf_op jit(solution)/shard_map/ppermute | solution.py:71
  68.6 8.5 %collective-permute-start.7 = (bf16[512,256]{0,1:T(8,128)(2,1)S(1)}, bf16[512,256]{0,1:T(8,128)(2,1)S(1)}, u32[]{:S(2)}, u32[]{:S(2)}) collective-permute-start(bf16[512,256]{0,1:T(8,128)(2,1)S(1)} %collective-permute-done.6), channel_id=1, source_target_pairs={{0,2},{2,4},{4,6},{6,8},{8,10},{10,12},{12,14},{14,16},{16,18},{18... | collective-permute-start | bytes 786440 | tf_op jit(solution)/shard_map/ppermute | solution.py:71
  77.8 8.5 %collective-permute-start.8 = (bf16[512,256]{0,1:T(8,128)(2,1)S(1)}, bf16[512,256]{0,1:T(8,128)(2,1)S(1)}, u32[]{:S(2)}, u32[]{:S(2)}) collective-permute-start(bf16[512,256]{0,1:T(8,128)(2,1)S(1)} %collective-permute-done.7), channel_id=1, source_target_pairs={{0,2},{2,4},{4,6},{6,8},{8,10},{10,12},{12,14},{14,16},{16,18},{18... | collective-permute-start | bytes 786440 | tf_op jit(solution)/shard_map/ppermute | solution.py:71
  87.0 8.5 %collective-permute-start.9 = (bf16[512,256]{0,1:T(8,128)(2,1)S(1)}, bf16[512,256]{0,1:T(8,128)(2,1)S(1)}, u32[]{:S(2)}, u32[]{:S(2)}) collective-permute-start(bf16[512,256]{0,1:T(8,128)(2,1)S(1)} %collective-permute-done.8), channel_id=1, source_target_pairs={{0,2},{2,4},{4,6},{6,8},{8,10},{10,12},{12,14},{14,16},{16,18},{18... | collective-permute-start | bytes 786440 | tf_op jit(solution)/shard_map/ppermute | solution.py:71
  96.2 8.5 %collective-permute-start.10 = (bf16[512,256]{0,1:T(8,128)(2,1)S(1)}, bf16[512,256]{0,1:T(8,128)(2,1)S(1)}, u32[]{:S(2)}, u32[]{:S(2)}) collective-permute-start(bf16[512,256]{0,1:T(8,128)(2,1)S(1)} %collective-permute-done.9), channel_id=1, source_target_pairs={{0,2},{2,4},{4,6},{6,8},{8,10},{10,12},{12,14},{14,16},{16,18},{18... | collective-permute-start | bytes 786440 | tf_op jit(solution)/shard_map/ppermute | solution.py:71
  105.4 8.5 %collective-permute-start.11 = (bf16[512,256]{0,1:T(8,128)(2,1)S(1)}, bf16[512,256]{0,1:T(8,128)(2,1)S(1)}, u32[]{:S(2)}, u32[]{:S(2)}) collective-permute-start(bf16[512,256]{0,1:T(8,128)(2,1)S(1)} %collective-permute-done.10), channel_id=1, source_target_pairs={{0,2},{2,4},{4,6},{6,8},{8,10},{10,12},{12,14},{14,16},{16,18},{18... | collective-permute-start | bytes 786440 | tf_op jit(solution)/shard_map/ppermute | solution.py:71
  114.6 14.0 %collective-permute-start.12 = (bf16[512,256]{0,1:T(8,128)(2,1)S(1)}, bf16[512,256]{0,1:T(8,128)(2,1)S(1)}, u32[]{:S(2)}, u32[]{:S(2)}) collective-permute-start(bf16[512,256]{0,1:T(8,128)(2,1)S(1)} %collective-permute-done.11), channel_id=1, source_target_pairs={{0,2},{2,4},{4,6},{6,8},{8,10},{10,12},{12,14},{14,16},{16,18},{18... | collective-permute-start | bytes 786440 | tf_op jit(solution)/shard_map/ppermute | solution.py:71
  129.3 8.7 %collective-permute-start.13 = (bf16[512,256]{0,1:T(8,128)(2,1)S(1)}, bf16[512,256]{0,1:T(8,128)(2,1)S(1)}, u32[]{:S(2)}, u32[]{:S(2)}) collective-permute-start(bf16[512,256]{0,1:T(8,128)(2,1)S(1)} %collective-permute-done.12), channel_id=1, source_target_pairs={{0,2},{2,4},{4,6},{6,8},{8,10},{10,12},{12,14},{14,16},{16,18},{18... | collective-permute-start | bytes 786440 | tf_op jit(solution)/shard_map/ppermute | solution.py:71
  138.7 12.9 %collective-permute-start.14 = (bf16[512,256]{0,1:T(8,128)(2,1)S(1)}, bf16[512,256]{0,1:T(8,128)(2,1)S(1)}, u32[]{:S(2)}, u32[]{:S(2)}) collective-permute-start(bf16[512,256]{0,1:T(8,128)(2,1)S(1)} %collective-permute-done.13), channel_id=1, source_target_pairs={{0,2},{2,4},{4,6},{6,8},{8,10},{10,12},{12,14},{14,16},{16,18},{18... | collective-permute-start | bytes 786440 | tf_op jit(solution)/shard_map/ppermute | solution.py:71
  138.7 15.1 %collective-permute-start = (bf16[256,64]{0,1:T(8,128)(2,1)S(1)}, bf16[256,64]{0,1:T(8,128)(2,1)S(1)}, u32[]{:S(2)}, u32[]{:S(2)}) collective-permute-start(bf16[256,64]{0,1:T(8,128)(2,1)S(1)} %get-tuple-element.13), channel_id=1, source_target_pairs={{0,1},{1,0},{2,3},{3,2},{4,5},{5,4},{6,7},{7,6},{8,9},{9,8},{10,11... | collective-permute-start | bytes 98312 | tf_op jit(solution)/shard_map/ppermute | solution.py:16
  151.6 10.7 %collective-permute-start.15 = (bf16[512,256]{0,1:T(8,128)(2,1)S(1)}, bf16[512,256]{0,1:T(8,128)(2,1)}, u32[]{:S(2)}, u32[]{:S(2)}) collective-permute-start(bf16[512,256]{0,1:T(8,128)(2,1)S(1)} %collective-permute-done.14), channel_id=1, source_target_pairs={{0,2},{2,4},{4,6},{6,8},{8,10},{10,12},{12,14},{14,16},{16,18},{18... | collective-permute-start | bytes 786440 | tf_op jit(solution)/shard_map/ppermute | solution.py:71
  154.5 107.7 %reduce-scatter.2.cloned.1.call-start = ((), (), s32[]{:S(2)}) async-start(), calls=%async_computation.5 | async-start | bytes 4718592 | tf_op jit(solution)/shard_map/reduce_scatter | solution.py:113
  162.3 8.8 %collective-permute-start.16 = (bf16[512,256]{0,1:T(8,128)(2,1)}, bf16[512,256]{0,1:T(8,128)(2,1)}, u32[]{:S(2)}, u32[]{:S(2)}) collective-permute-start(bf16[512,256]{0,1:T(8,128)(2,1)} %collective-permute-done.15), channel_id=1, source_target_pairs={{0,2},{2,4},{4,6},{6,8},{8,10},{10,12},{12,14},{14,16},{16,18},{18... | collective-permute-start | bytes 786440 | tf_op jit(solution)/shard_map/ppermute | solution.py:71
  162.4 22.6 %copy-start.12 = (bf16[512,256]{0,1:T(8,128)(2,1)S(1)}, bf16[512,256]{0,1:T(8,128)(2,1)}, u32[]{:S(2)}) copy-start(bf16[512,256]{0,1:T(8,128)(2,1)} %copy-done.11) | copy-start | bytes 786436
  162.4 23.3 %copy-start.10 = (bf16[512,256]{0,1:T(8,128)(2,1)S(1)}, bf16[512,256]{0,1:T(8,128)(2,1)}, u32[]{:S(2)}) copy-start(bf16[512,256]{0,1:T(8,128)(2,1)} %copy-done.9) | copy-start | bytes 786436
  162.4 24.0 %copy-start.8 = (bf16[512,256]{0,1:T(8,128)(2,1)S(1)}, bf16[512,256]{0,1:T(8,128)(2,1)}, u32[]{:S(2)}) copy-start(bf16[512,256]{0,1:T(8,128)(2,1)} %copy-done.7) | copy-start | bytes 786436
  162.4 24.7 %copy-start.6 = (bf16[512,256]{0,1:T(8,128)(2,1)S(1)}, bf16[512,256]{0,1:T(8,128)(2,1)}, u32[]{:S(2)}) copy-start(bf16[512,256]{0,1:T(8,128)(2,1)} %copy-done.5) | copy-start | bytes 786436
  162.4 25.4 %copy-start.4 = (bf16[512,256]{0,1:T(8,128)(2,1)S(1)}, bf16[512,256]{0,1:T(8,128)(2,1)}, u32[]{:S(2)}) copy-start(bf16[512,256]{0,1:T(8,128)(2,1)} %copy-done.3) | copy-start | bytes 786436
  162.4 31.0 %copy-start.25 = (bf16[512,256]{0,1:T(8,128)(2,1)S(1)}, bf16[512,256]{0,1:T(8,128)(2,1)}, u32[]{:S(2)}) copy-start(bf16[512,256]{0,1:T(8,128)(2,1)} %copy-done.24) | copy-start | bytes 786436
  162.4 31.7 %copy-start.23 = (bf16[512,256]{0,1:T(8,128)(2,1)S(1)}, bf16[512,256]{0,1:T(8,128)(2,1)}, u32[]{:S(2)}) copy-start(bf16[512,256]{0,1:T(8,128)(2,1)} %copy-done.22) | copy-start | bytes 786436
  162.4 32.4 %copy-start.21 = (bf16[512,256]{0,1:T(8,128)(2,1)S(1)}, bf16[512,256]{0,1:T(8,128)(2,1)}, u32[]{:S(2)}) copy-start(bf16[512,256]{0,1:T(8,128)(2,1)} %copy-done.20) | copy-start | bytes 786436
  166.3 26.3 %copy-start.27 = (bf16[512,256]{0,1:T(8,128)(2,1)S(1)}, bf16[512,256]{0,1:T(8,128)(2,1)}, u32[]{:S(2)}) copy-start(bf16[512,256]{0,1:T(8,128)(2,1)} %copy-done.26) | copy-start | bytes 786436
  166.3 37.5 %copy-start.1 = (bf16[384,4096]{1,0:T(8,128)(2,1)S(1)}, bf16[384,4096]{1,0:T(8,128)(2,1)}, u32[]{:S(2)}) copy-start(bf16[384,4096]{1,0:T(8,128)(2,1)} %all-gather.7.cloned.1.call-done) | copy-start | bytes 9437188
  (18 other events, 106.0 us)
Sparse Core Ops, SparseCore 0:
  14.9 39.7 all-gather.8
  56.2 46.5 all-gather.6
  105.0 54.7 all-gather.10
  161.8 36.8 all-gather.4
  221.5 40.5 reduce-scatter.1
